TPU v7x, 128 devices: a whole 4x4x4 slice. The times are simulated.
128 devices in a mesh: dp: 32 (over y, x, core), tensor: 4 (over z).
Axes of the slice: x: 4, y: 4, z: 4, core: 2. Of those that a mesh axis runs over, the one named last changes fastest.
Arguments:
- hidden_states: bfloat16 [12288, 8192], P('dp'), may hold values from -6 to 6
- teacher_weight: bfloat16 [8192, 4096], P('dp', 'tensor'), may hold values from -0.088388348 to 0.088388348
- student_blocks: bfloat16 [192, 4, 128, 128], P('dp', 'tensor'), may hold values from -0.125 to 0.125
- block_index: int32 [192, 4], P('dp', 'tensor'), may hold values from -1 to 15, as said below
Outputs:
- block_grads: float32 [192, 4, 128, 128], P('dp', 'tensor')
- input_grad: bfloat16 [12288, 8192], P('dp', 'tensor')
Inputs may be any that keep to these rules, and one draw needn't show every extreme that they name: `block_index`: entries (i * 6 + s, j) for s < 6 form one shard's list: its live entries are distinct block numbers of the shard's 2 x 8 blocks, they come first and the rest are -1; every shard has 3 to 6 live entries, and in every draw some shard has exactly 6.
All inputs are finite; a program needn't handle non-finite values.
Results may differ from a plain program's by a relative error of at most 0.014.
Values may be sent and summed in bfloat16 or wider, within the bound.
A program may use at most 192 MiB of HBM per device.

v0:
```python
import math

import jax
import jax.numpy as jnp
from jax import lax
from jax.sharding import PartitionSpec as P


def scatter_blocks(values, index, shards, row_blocks, col_blocks, per_shard):
    size = values.shape[-1]
    live = index >= 0
    safe = jnp.maximum(index, 0)
    owner = jnp.arange(index.shape[0], dtype=jnp.int32) // per_shard
    rows = owner * row_blocks + safe // col_blocks
    cols = safe % col_blocks
    masked = jnp.where(live[:, None, None], values, jnp.zeros_like(values))
    grid = jnp.zeros((shards * row_blocks, size, col_blocks, size), values.dtype)
    grid = grid.at[rows, :, cols, :].add(masked)
    return grid.reshape(shards * row_blocks * size, col_blocks * size)


def body(hidden_states, teacher_weight, student_blocks, block_index):
    tok_rows = hidden_states.shape[0]
    model_width = hidden_states.shape[1]
    block = student_blocks.shape[-1]
    per_shard = student_blocks.shape[0]
    shard_rows = teacher_weight.shape[0]
    local_width = teacher_weight.shape[1]
    row_blocks = shard_rows // block
    col_blocks = local_width // block
    total_tokens = tok_rows * lax.axis_size("dp")
    width_all = local_width * lax.axis_size("tensor")
    columns = hidden_states
    teacher_out = jnp.dot(
        columns,
        lax.all_gather(teacher_weight, "dp", axis=0, tiled=True),
        preferred_element_type=jnp.float32,
    )

    def slab_of(pieces, start):
        shards = pieces[0].shape[0] // per_shard
        slab = scatter_blocks(
            pieces[0][:, 0], pieces[1][:, 0], shards, row_blocks, col_blocks, per_shard
        )
        return (slab, start // per_shard * shard_rows)

    index_init = jnp.zeros((per_shard * lax.axis_size("dp"), 1), jnp.int32)
    pieces = (
        lax.all_gather(student_blocks, "dp", axis=0, tiled=True),
        lax.all_gather(block_index, "dp", axis=0, tiled=True),
    )
    start = jnp.int32(0)
    student_index_all = index_init
    slab, row_start = slab_of(pieces, start)
    columns = hidden_states
    total = jnp.dot(columns, slab, preferred_element_type=jnp.float32)
    student_index_all = lax.dynamic_update_slice_in_dim(student_index_all, pieces[1], start, 0)
    squares = jnp.sum(teacher_out * teacher_out, axis=1)
    squares = lax.psum(squares, "tensor")
    weight = 1.0 / (squares / width_all + 1e-05)
    scale = 1.0 / math.sqrt(total_tokens)
    grad_out = (weight[:, None] * (total - teacher_out) * scale).astype(jnp.bfloat16)
    inputs3 = hidden_states.reshape(tok_rows, model_width // block, block)
    grads3 = grad_out.reshape(tok_rows, col_blocks, block)
    listed = student_index_all[:, 0]
    alive = listed >= 0
    safe = jnp.maximum(listed, 0)
    owner = jnp.arange(lax.axis_size("dp") * per_shard, dtype=jnp.int32) // per_shard
    rows = owner * row_blocks + safe // col_blocks
    cols = safe % col_blocks
    left = jnp.take(inputs3, rows, axis=1)
    right = jnp.take(grads3, cols, axis=1)
    term = jnp.einsum("tkd,tke->kde", left, right, preferred_element_type=jnp.float32)
    term = jnp.where(alive[:, None, None], term, jnp.zeros_like(term))
    block_grads = lax.psum_scatter(
        term[:, None].astype(jnp.bfloat16), "dp", scatter_dimension=0, tiled=True
    ).astype(jnp.float32)
    slab, row_start = slab_of(
        (
            lax.all_gather(student_blocks, "dp", axis=0, tiled=True),
            lax.all_gather(block_index, "dp", axis=0, tiled=True),
        ),
        jnp.int32(0),
    )
    part_grad = lax.dot_general(
        grad_out, slab, (((1,), (1,)), ((), ())), preferred_element_type=jnp.float32
    )
    input_grad = lax.psum_scatter(
        part_grad.astype(jnp.bfloat16), "tensor", scatter_dimension=1, tiled=True
    )
    return (block_grads, input_grad)


def solution(mesh):
    in_specs = (P("dp", None), P("dp", "tensor"), P("dp", "tensor", None, None), P("dp", "tensor"))
    out_specs = (P("dp", "tensor", None, None), P("dp", "tensor"))
    return jax.shard_map(body, mesh=mesh, in_specs=in_specs, out_specs=out_specs, check_vma=False)
```

profile of v0, /device:TPU:1, one launch (start us, length us, event | category | flops | bytes accessed | tf_op | source)
XLA Modules:
  0.0 356.9 jit_solution(5125436822623616376)
XLA Ops:
  7.2 0.0 all-gather.5.cloned.1.call-start
  7.2 0.7 all-gather.5.cloned.1.call-update
  7.9 0.0 all-gather.3.cloned.1.call-start
  7.9 0.7 all-gather.3.cloned.1.call-update
  8.6 0.0 reduce-scatter.3.cloned.1.call-start
  8.7 8.7 %copy.24 = bf16[384,8192]{0,1:T(8,128)(2,1)} copy(bf16[384,8192]{1,0:T(8,128)(2,1)} %param.4) | data formatting | bytes 12582912 | tf_op args[0]
  17.4 8.7 %copy.25 = bf16[384,64,128]{2,0,1:T(8,128)(2,1)} copy(bf16[384,64,128]{0,2,1:T(8,128)(2,1)} %bitcast.55) | data formatting | bytes 12582912 | tf_op jit(solution)/shard_map/reshape | solution.py:63
  26.1 0.0 copy-done.2
  26.1 0.6 dynamic-slice
  27.4 0.1 bitcast_dynamic-update-slice_fusion
  27.5 14.9 %all-reduce = s32[192]{0:T(256)S(1)} all-reduce(s32[192]{0:T(256)S(1)} %bitcast_dynamic-update-slice_fusion), channel_id=1, replica_groups=mesh['dp'=32,'tensor'=4] {'dp'}, use_global_device_ids=true, to_apply=%add | all-reduce | flops 192 | bytes 1536
  42.4 13.9 %gather_fusion = bf16[192,384,128]{2,1,0:T(8,128)(2,1)} fusion(bf16[384,64,128]{2,0,1:T(8,128)(2,1)} %copy.25, s32[1024]{0:T(1024)S(1)} %pad_clamp_fusion.1), kind=kCustom, calls=%fused_computation | custom fusion | bytes 37749504 | tf_op jit(solution)/shard_map/jit(_take)/gather | solution.py:71
  56.3 6.6 %all-gather.5.cloned.1.call-done = bf16[192,1,128,128]{3,2,1,0:T(8,128)(2,1)} async-done(((bf16[6,1,128,128]{3,2,1,0:T(8,128)(2,1)}), bf16[192,1,128,128]{3,2,1,0:T(8,128)(2,1)}) %all-gather.5.cloned.1.call-update) | async-done | bytes 6291472 | tf_op jit(solution)/shard_map/all_gather | solution.py:49
  62.9 6.0 %bitcast_select_fusion = bf16[192,128,128]{2,1,0:T(8,128)(2,1)} fusion(bf16[192,1,128,128]{3,2,1,0:T(8,128)(2,1)} %all-gather.5.cloned.1.call-done, pred[192]{0:T(512)(128)(4,1)S(1)} %get-tuple-element.17), kind=kLoop, calls=%fused_computation.20 | loop fusion | flops 3145728 | bytes 12583104 | tf_op jit(solution)/shard_map/jit(_where)/select_n | solution.py:16
  68.9 6.4 %broadcast.131 = bf16[64,128,8,128]{3,1,2,0:T(8,128)(2,1)} broadcast(bf16[]{:T(256)} %constant.98.clone.1), dimensions={} | broadcast | bytes 16777218 | tf_op jit(solution)/shard_map/broadcast.10
  75.3 40.1 %scatter_fusion = bf16[64,128,8,128]{3,1,2,0:T(8,128)(2,1)} fusion(bf16[64,128,8,128]{3,1,2,0:T(8,128)(2,1)} %broadcast.131, s32[192]{0:T(256)S(1)} %bitcast.58, bf16[192,128,128]{2,1,0:T(8,128)(2,1)} %bitcast_select_fusion), kind=kCustom, calls=%fused_computation.2 | custom fusion | flops 3145728 | bytes 18875904 | tf_op jit(solution)/shard_map/scatter-add | solution.py:18
  115.4 19.7 %copy.26 = bf16[64,128,8,128]{3,2,1,0:T(8,128)(2,1)} copy(bf16[64,128,8,128]{3,1,2,0:T(8,128)(2,1)} %scatter_fusion) | data formatting | bytes 33554432 | tf_op jit(solution)/shard_map/scatter-add | solution.py:18
  135.1 0.0 slice-done.1
  135.1 11.5 %fusion.9 = f32[1024,384]{0,1:T(8,128)} fusion(bf16[384,8192]{1,0:T(8,128)(2,1)S(1)} %bitcast.60, bf16[1024,8,8,128]{3,2,1,0:T(8,128)(2,1)} %bitcast.56), kind=kOutput, calls=%fused_computation.12 | convolution fusion | flops 6442450944 | bytes 24641536 | tf_op jit(solution)/shard_map/dot_general | solution.py:56
  146.6 13.1 %multiply_reduce_fusion = (f32[384]{0:T(512)S(1)}, f32[384,1024]{1,0:T(8,128)}) fusion(bf16[384,8192]{1,0:T(8,128)(2,1)} %param.4, bf16[8192,1024]{1,0:T(8,128)(2,1)} %all-gather.3.cloned.1.call-done), kind=kOutput, calls=%fused_computation.26 | convolution fusion | flops 6443236864 | bytes 24643072 | tf_op jit(solution)/shard_map/dot_general | solution.py:34
  159.7 8.8 %psum.7 = f32[384]{0:T(512)S(1)} all-reduce(f32[384]{0:T(512)S(1)} %get-tuple-element.20), channel_id=1, replica_groups=mesh['dp'=32,'tensor'=4] {'tensor'}, use_global_device_ids=true, to_apply=%region_1.2 | all-reduce | flops 384 | bytes 3072 | tf_op jit(solution)/shard_map/psum | solution.py:59
  168.5 0.0 copy-done
  168.5 1.8 copy_bitcast_fusion
  170.3 10.2 %gather_fusion.1 = bf16[192,384,128]{2,1,0:T(8,128)(2,1)} fusion(bf16[384,8,128]{2,0,1:T(8,128)(2,1)S(1)} %copy_bitcast_fusion, s32[1024]{0:T(1024)S(1)} %pad_clamp_fusion), kind=kCustom, calls=%fused_computation.1 | custom fusion | bytes 37749504 | tf_op jit(solution)/shard_map/jit(_take)/gather | solution.py:72
  180.5 18.1 %fusion.17 = bf16[192,1,128,128]{3,2,0,1:T(8,128)(2,1)} fusion(pred[192]{0:T(512)(128)(4,1)S(1)} %get-tuple-element.17, bf16[192,384,128]{2,1,0:T(8,128)(2,1)} %gather_fusion.1, pred[192]{0:T(512)(128)(4,1)S(1)} %get-tuple-element.14, bf16[192,384,128]{2,1,0:T(8,128)(2,1)} %gather_fusion, pred[192]{0:T(512)(128)(4,1)S(1)} %get-tuple-element.10), kind=kOutput, calls=%fused_computation.19 | convolution fusion | flops 2441084928 | bytes 44040768 | tf_op jit(solution)/shard_map/tkd,tke->kde/dot_general | solution.py:73
  198.6 0.0 reduce-scatter.3.cloned.1.call-update
  198.6 0.0 reduce-scatter.5.cloned.1.call-start
  198.7 12.6 %fusion.13 = bf16[384,8192]{1,0:T(8,128)(2,1)} fusion(bf16[1024,8,8,128]{3,2,1,0:T(8,128)(2,1)} %bitcast.57, f32[384,1024]{1,0:T(8,128)} %get-tuple-element.21, f32[1024,384]{0,1:T(8,128)S(1)} %copy-done, f32[384]{0:T(512)S(1)} %add_divide_fusion), kind=kOutput, calls=%fused_computation.17 | convolution fusion | flops 6447169536 | bytes 26215936 | tf_op jit(solution)/shard_map/dot_general | solution.py:85
  211.3 0.0 reduce-scatter.5.cloned.1.call-update
  211.3 70.8 %reduce-scatter.3.cloned.1.call-done = bf16[6,1,128,128]{3,2,0,1:T(8,128)(2,1)} async-done(((bf16[192,1,128,128]{3,2,0,1:T(8,128)(2,1)}), bf16[6,1,128,128]{3,2,0,1:T(8,128)(2,1)}) %reduce-scatter.3.cloned.1.call-update) | async-done | bytes 196624 | tf_op jit(solution)/shard_map/reduce_scatter | solution.py:75
  282.1 1.7 bitcast_convert_fusion
  283.8 66.6 %reduce-scatter.5.cloned.1.call-done = bf16[384,2048]{1,0:T(8,128)(2,1)} async-done(((bf16[384,8192]{1,0:T(8,128)(2,1)}), bf16[384,2048]{1,0:T(8,128)(2,1)}) %reduce-scatter.5.cloned.1.call-update) | async-done | bytes 1572880 | tf_op jit(solution)/shard_map/reduce_scatter | solution.py:88
  (17 shorter events, 0.1 us)
Async XLA Ops:
  7.2 55.7 %all-gather.5.cloned.1.call-start = ((), (), s32[]{:S(2)}) async-start(), calls=%async_computation.3 | async-start | bytes 6488064 | tf_op jit(solution)/shard_map/all_gather | solution.py:49
  7.9 138.7 %all-gather.3.cloned.1.call-start = ((), (), s32[]{:S(2)}) async-start(), calls=%async_computation.2 | async-start | bytes 17301504 | tf_op jit(solution)/shard_map/all_gather | solution.py:36
  8.6 273.5 %reduce-scatter.3.cloned.1.call-start = ((), (), s32[]{:S(2)}) async-start(), calls=%async_computation.4 | async-start | bytes 6488064 | tf_op jit(solution)/shard_map/reduce_scatter | solution.py:75
  17.4 8.7 %copy-start.2 = (u32[128]{0:T(128)S(1)}, u32[128]{0:T(128)}, u32[]{:S(2)}) copy-start(u32[128]{0:T(128)} %constant.120) | copy-start | bytes 1540
  17.4 10.0 %copy-start.1 = (s32[6,1]{0,1:T(1,128)S(1)}, s32[6,1]{0,1:T(1,128)}, u32[]{:S(2)}) copy-start(s32[6,1]{0,1:T(1,128)} %param.7) | copy-start | bytes 76
  75.3 59.8 %slice-start = ((s8[6291456]{0:T(1024)(128)(4,1)}), s8[2097152]{0:T(1024)(128)(4,1)S(1)}, s32[]{:S(2)}) async-start(s8[6291456]{0:T(1024)(128)(4,1)} %bitcast.59), calls=%async_computation.6 | async-start | bytes 4194304
  115.4 19.7 %slice-start.1 = ((s8[6291456]{0:T(1024)(128)(4,1)}), s8[4194304]{0:T(1024)(128)(4,1)S(1)}, s32[]{:S(2)}) async-start(s8[6291456]{0:T(1024)(128)(4,1)} %bitcast.59), calls=%async_computation.7 | async-start | bytes 8388608
  146.6 21.9 %copy-start = (f32[1024,384]{0,1:T(8,128)S(1)}, f32[1024,384]{0,1:T(8,128)}, u32[]{:S(2)}) copy-start(f32[1024,384]{0,1:T(8,128)} %fusion.9) | copy-start | bytes 4718596
  198.6 151.8 %reduce-scatter.5.cloned.1.call-start = ((), (), s32[]{:S(2)}) async-start(), calls=%async_computation.5 | async-start | bytes 7864320 | tf_op jit(solution)/shard_map/reduce_scatter | solution.py:88
Sparse Core Ops, SparseCore 0:
  10.2 52.6 all-gather.4
  65.2 71.3 all-gather.2
  198.8 83.3 reduce-scatter.2
  285.1 65.2 reduce-scatter.4
where the time goes:
time: 358 us; the launch traced here: 357 us
  waiting for transfers between devices  145 us (41%)
  local copies, waits for them, and re-layouts  68.3 us (19%)
  matrix products  55.3 us (15%)
  other arithmetic  49.7 us (14%)
  blocking collectives  23.7 us (7%)
  between operations  14.5 us (4%)
    reduce_scatter x1, waiting for transfers between devices, body(): lax.psum_scatter(term[:, None].astype(jnp.bfloat16), 'dp', scatter_dimens...  70.8 us
    reduce_scatter x1, waiting for transfers between devices, body(): lax.psum_scatter(part_grad.astype(jnp.bfloat16), 'tensor', scatter_dimens...  66.6 us
    scatter-add x1, other arithmetic, scatter_blocks(): grid = grid.at[rows, :, cols, :].add(masked)  40.1 us
    scatter-add x1, local copies, waits for them, and re-layouts, scatter_blocks(): grid = grid.at[rows, :, cols, :].add(masked)  19.7 us
    dot_general x1, matrix products, body(): jnp.einsum('tkd,tke->kde', left, right, preferred_element_type=jnp.float32)  18.1 us
    unnamed x1, blocking collectives  14.9 us
    gather x1, local copies, waits for them, and re-layouts, body(): left = jnp.take(inputs3, rows, axis=1)  13.9 us
    dot_general x1, matrix products, body(): jnp.dot(columns, lax.all_gather(teacher_weight, 'dp', axis=0, tiled=True)...  13.1 us
  transfers between devices with their start and end apart: 4, of which 3 were waited for; matrix products, arithmetic and copies ran while one was open for 36% of the time, Pallas kernels for 0%

commit v1 on v0

v1 whole, which is shorter than its diff:
```python
import functools
import math

import jax
import jax.numpy as jnp
from jax import lax
from jax.experimental import pallas as pl
from jax.experimental.pallas import tpu as pltpu
from jax.sharding import PartitionSpec as P

MESH = pl.DeviceIdType.MESH
F32 = jnp.float32
BF16 = jnp.bfloat16
TOK = 384
D = 8192
BLK = 128
CAP = 6
COLS = 1024
HALF = 512
OWN_COLS = 2048
BROWS = CAP * BLK
TOKENS = 12288
QW = 4096
U_OF_K = (0, -1, 1, 2)


class Payload:
    def __init__(self, env, buf, sems):
        self.env = env
        self.buf = buf
        self.rows = buf.shape[2]
        self.send, self.recv, self.sib_send, self.sib_recv = sems

    def off(self, lane, du, dv):
        return (du, dv) if lane == 0 else (dv, du)

    def piece(self, core, dx, dy, lane, q0, nq):
        quarter = self.rows // 4
        return self.buf.at[self.env.chip(dx, dy), core, pl.ds((lane * 2 + q0) * quarter, nq * quarter), :]

    def copy(self, lane, du, dv, q0, nq, axis, sign, event):
        dx, dy = self.off(lane, du, dv)
        ref = self.piece(self.env.core, dx, dy, lane, q0, nq)
        step = self.off(lane, sign, 0) if axis == 0 else self.off(lane, 0, sign)
        return pltpu.make_async_remote_copy(
            src_ref=ref,
            dst_ref=ref,
            send_sem=self.send.at[lane, event],
            recv_sem=self.recv.at[lane, event],
            device_id=self.env.peer(*step),
            device_id_type=MESH,
        )

    def put(self, *args):
        c = self.copy(*args)
        c.start()
        self.env.started.append(c)

    def got(self, lane, du, dv, q0, nq, event):
        self.copy(lane, du, dv, q0, nq, 0, 1, event).wait_recv()

    def sib_copy(self, core, lane, dx, dy):
        ref = self.piece(core, dx, dy, lane, 0, 2)
        at = lane * 16 + (dx % 4) * 4 + dy % 4
        return pltpu.make_async_remote_copy(
            src_ref=ref,
            dst_ref=ref,
            send_sem=self.sib_send.at[at],
            recv_sem=self.sib_recv.at[at],
            device_id=self.env.sibling,
            device_id_type=MESH,
        )

    def to_sibling(self, lane, du, dv):
        c = self.sib_copy(self.env.core, lane, *self.off(lane, du, dv))
        c.start()
        self.env.started.append(c)

    def from_sibling(self, dx, dy):
        for lane in (0, 1):
            self.sib_copy(1 - self.env.core, lane, dx, dy).wait_recv()

    def own(self):
        for lane in (0, 1):
            for axis, base in ((0, 0), (1, 4)):
                self.put(lane, 0, 0, 0, 2, axis, 1, base)
                self.put(lane, 0, 0, 0, 2, axis, -1, base + 1)
        for lane in (0, 1):
            self.to_sibling(lane, 0, 0)

    def u1(self, lane):
        for k, du, sign, event in ((1, -1, 1, 0), (2, 1, -1, 1)):
            self.got(lane, du, 0, 0, 2, event)
            self.put(lane, du, 0, event, 1, 0, sign, 2 + event)
            self.put(lane, du, 0, 0, 2, 1, 1, 4 + 4 * k)
            self.put(lane, du, 0, 0, 2, 1, -1, 5 + 4 * k)
            self.to_sibling(lane, du, 0)

    def u2(self, lane):
        self.got(lane, 2, 0, 0, 1, 2)
        self.got(lane, 2, 0, 1, 1, 3)
        self.put(lane, 2, 0, 0, 2, 1, 1, 16)
        self.put(lane, 2, 0, 0, 2, 1, -1, 17)
        self.to_sibling(lane, 2, 0)

    def v1(self, lane, k):
        du = U_OF_K[k]
        for dv, sign, event in ((-1, 1, 0), (1, -1, 1)):
            self.got(lane, du, dv, 0, 2, 4 + 4 * k + event)
            self.put(lane, du, dv, event, 1, 1, sign, 6 + 4 * k + event)
            self.to_sibling(lane, du, dv)

    def v2(self, lane, k):
        du = U_OF_K[k]
        self.got(lane, du, 2, 0, 1, 6 + 4 * k)
        self.got(lane, du, 2, 1, 1, 7 + 4 * k)
        self.to_sibling(lane, du, 2)

    def events(self):
        both = lambda f, *a: [functools.partial(f, 0, *a), functools.partial(f, 1, *a)]
        seq = []
        seq += both(self.u1) + both(self.v1, 0)
        seq += both(self.u2)
        seq += both(self.v1, 1) + both(self.v1, 2)
        seq += both(self.v2, 0) + both(self.v1, 3)
        seq += both(self.v2, 1) + both(self.v2, 2) + both(self.v2, 3)
        return seq


DONE_AFTER = {
    3: ((-1, 0), (1, 0), (0, -1), (0, 1)),
    9: ((-1, -1), (-1, 1), (1, -1), (1, 1)),
    11: ((2, 0), (0, 2)),
    17: ((2, -1), (2, 1), (-1, 2), (1, 2)),
    19: ((2, 2),),
}
CHIP_ORDER = ((0, 0),) + DONE_AFTER[3] + DONE_AFTER[9] + DONE_AFTER[11] + DONE_AFTER[17] + DONE_AFTER[19]
GRAD_ORDER = (
    (2, 2), (2, 1), (2, -1), (1, 2), (-1, 2), (2, 0), (0, 2), (1, 1),
    (1, -1), (-1, 1), (-1, -1), (1, 0), (-1, 0), (0, 1), (0, -1), (0, 0),
)


class Env:
    pass


def rel(dx, dy):
    return (dx % 4) * 4 + dy % 4


def kernel(
    x_hbm, w_hbm, b_hbm, i_hbm, gout, iout,
    xv, wv, bv, fv, idxv, idxs, acc_t, acc_s, few, slab, dv, gt, dense, pv, ss, sr, rv1, rv2, ru1, ru2, sqv, wcol, iacc,
    loc_sem, p_send, p_recv, p_sib_send, p_sib_recv,
    i_send, i_recv, f_send, f_recv, d_send, d_recv, q_send, q_recv, g_send, g_recv, r_send, r_recv,
):
    dp = lax.axis_index("dp")
    z = lax.axis_index("tensor")
    core = lax.rem(dp, 2)
    x = lax.rem(dp // 2, 4)
    y = dp // 8
    env = Env()
    env.core = core
    env.started = []

    def mod4(a, d):
        return a if d == 0 else lax.rem(a + (d % 4), 4)

    env.chip = lambda dx, dy: mod4(y, dy) * 4 + mod4(x, dx)
    env.peer = lambda dx, dy: (env.chip(dx, dy) * 2 + core, z)
    env.sibling = (env.chip(0, 0) * 2 + 1 - core, z)
    zpeer = lambda d: (dp, mod4(z, d))

    def remote(src, dst, send, recv, device):
        return pltpu.make_async_remote_copy(
            src_ref=src, dst_ref=dst, send_sem=send, recv_sem=recv, device_id=device, device_id_type=MESH
        )

    def go(c):
        c.start()
        env.started.append(c)

    here = env.chip(0, 0)
    own_b = pltpu.make_async_copy(b_hbm, bv.at[here, core], loc_sem.at[0])
    own_i = pltpu.make_async_copy(i_hbm, idxv.at[core, y, x, z], loc_sem.at[1])
    own_w = [
        pltpu.make_async_copy(w_hbm.at[:, pl.ds(HALF * h, HALF)], wv.at[h, here, core], loc_sem.at[2 + h])
        for h in (0, 1)
    ]
    own_x = pltpu.make_async_copy(x_hbm, xv, loc_sem.at[4])
    own_b.start()
    own_i.start()
    for c in own_w:
        c.start()
    own_x.start()

    barrier = pltpu.get_barrier_semaphore()
    peers = [env.sibling]
    peers += [env.peer(d, 0) for d in (1, 2, 3)] + [env.peer(0, d) for d in (1, 2, 3)] + [zpeer(d) for d in (1, 2, 3)]
    for p in peers:
        pl.semaphore_signal(barrier, inc=1, device_id=p, device_id_type=MESH)
    pl.semaphore_wait(barrier, len(peers))

    blocks, teach0, teach1 = [
        Payload(env, buf, (p_send.at[n], p_recv.at[n], p_sib_send.at[n], p_sib_recv.at[n]))
        for n, buf in ((0, bv), (1, wv.at[0]), (2, wv.at[1]))
    ]
    teach = (teach0, teach1)

    own_i.wait()
    own_b.wait()

    def idx_copies(stage):
        if stage == 0:
            ref = idxv.at[core, y, x, z]
            return [remote(ref, ref, i_send.at[d - 1], i_recv.at[d - 1], zpeer(d)) for d in (1, 2, 3)]
        if stage == 1:
            ref = idxv.at[core, y, x]
            return [remote(ref, ref, i_send.at[2 + d], i_recv.at[2 + d], env.peer(d, 0)) for d in (1, 2, 3)]
        if stage == 2:
            ref = idxv.at[core, y]
            return [remote(ref, ref, i_send.at[5 + d], i_recv.at[5 + d], env.peer(0, d)) for d in (1, 2, 3)]
        ref = idxv.at[core]
        return [remote(ref, ref, i_send.at[9], i_recv.at[9], env.sibling)]

    def idx_start(stage):
        for c in idx_copies(stage):
            go(c)

    def idx_wait(stage):
        for n in range(3 if stage < 3 else 1):
            d = n + 1
            if stage == 0:
                ref = idxv.at[core, y, x, mod4(z, -d)]
            elif stage == 1:
                ref = idxv.at[core, y, mod4(x, -d)]
            elif stage == 2:
                ref = idxv.at[core, mod4(y, -d)]
            else:
                ref = idxv.at[1 - core]
            at = 3 * stage + n
            remote(ref, ref, i_send.at[at], i_recv.at[at], env.sibling).wait_recv()

    idx_start(0)
    blocks.own()
    own_w[0].wait()
    teach0.own()
    idx_wait(0)
    idx_start(1)
    own_w[1].wait()
    own_x.wait()
    acc_t[...] = jnp.zeros_like(acc_t)
    acc_s[...] = jnp.zeros_like(acc_s)
    ev = blocks.events()
    for n, f in enumerate(ev):
        f()
        if n == 1:
            idx_wait(1)
            idx_start(2)
        if n == 5:
            idx_wait(2)
            idx_start(3)
        if n == 9:
            idx_wait(3)
            to_smem = pltpu.make_async_copy(idxv, idxs, loc_sem.at[5])
            to_smem.start()
            to_smem.wait()

    def f_copy(d, half):
        src = bv.at[pl.ds(mod4(z, d) * 4 + half * 2, 2), core]
        dst = fv.at[3 - d, pl.ds(half * 2, 2), core]
        at = (d - 1) * 2 + half
        return remote(src, dst, f_send.at[at], f_recv.at[at], zpeer(d))

    for d in (1, 3, 2):
        for half in (0, 1):
            go(f_copy(d, half))

    def f_sib(r, core_of):
        ref = fv.at[r, :, core_of]
        return remote(ref, ref, f_send.at[6 + r], f_recv.at[6 + r], env.sibling)

    def f_arrived(d):
        for half in (0, 1):
            f_copy(d, half).wait_recv()
        go(f_sib(3 - d, core))

    for dx, dy in CHIP_ORDER:
        blocks.from_sibling(dx, dy)

    for cc in (0, 1):
        few[cc, CAP] = jnp.zeros((BLK, BLK), BF16)
        dense[cc, 16] = jnp.zeros((BLK, BLK), BF16)

    def build(src, places):
        for cc in (0, 1):
            few[cc, 0:CAP] = src(cc).reshape(CAP, BLK, BLK)
            for q in range(16):
                slab[cc * 256 + q // 8 * BLK:cc * 256 + (q // 8 + 1) * BLK, q % 8 * BLK:(q % 8 + 1) * BLK] = few[
                    cc, places(cc, 8 + q)
                ]

    def columns_of(chip):
        return pl.ds(pl.multiple_of(chip * 512, 512), 512)

    def student(n):
        chip = n
        cy, cx = n // 4, n % 4
        build(
            lambda cc: bv[chip, cc],
            lambda cc, lane: idxs[cc, cy, cx, z, 0, lane],
        )
        for h in (0, 1):
            for t in (0, 1):
                acc_s[h, :, t * 256:(t + 1) * 256] += jnp.dot(
                    xv[:, chip * 512:(chip + 1) * 512],
                    slab[:, h * HALF + t * 256:h * HALF + (t + 1) * 256],
                    preferred_element_type=F32,
                )

    def teacher(h, dx, dy):
        teach[h].from_sibling(dx, dy)
        chip = env.chip(dx, dy)
        cols = columns_of(chip)
        for t in (0, 1):
            acc_t[h, :, t * 256:(t + 1) * 256] += jnp.dot(
                xv[:, cols],
                wv[h, chip, :, :, t * 256:(t + 1) * 256].reshape(512, 256),
                preferred_element_type=F32,
            )

    def d_copy(h, dist, event):
        rows = ((0, TOK), (0, TOK), (0, TOK // 2), (TOK // 2, TOK // 2))[event]
        ref = dv.at[h, mod4(z, dist), pl.ds(*rows), :]
        return remote(ref, ref, d_send.at[h, event], d_recv.at[h, event], zpeer(1 if event in (0, 2) else -1))

    def finish_half(h):
        t = acc_t[h]
        s = t * t
        s = s[:, 0:128] + s[:, 128:256] + s[:, 256:384] + s[:, 384:512]
        if h == 0:
            wcol[...] = s
        else:
            wcol[...] += s
        diff = acc_s[h] - t
        acc_s[h] = diff
        dv[h, z] = diff.astype(BF16)
        go(d_copy(h, 0, 0))
        go(d_copy(h, 0, 1))

    def d_forward(h):
        d_copy(h, -1, 0).wait_recv()
        go(d_copy(h, -1, 2))
        d_copy(h, 1, 1).wait_recv()
        go(d_copy(h, 1, 3))

    def d_last(h):
        d_copy(h, 2, 2).wait_recv()
        d_copy(h, 2, 3).wait_recv()

    def input_grad(n, dist, halves, first):
        plane = mod4(z, dist)
        if dist == 0:
            src = lambda cc: bv[z * 4 + n, cc]
        else:
            src = lambda cc: fv[dist - 1, n, cc]
        build(src, lambda cc, lane: idxs[cc, z, n, plane, 0, lane])
        for t in (0, 1):
            at = slice(n * 512 + t * 256, n * 512 + (t + 1) * 256)
            total = None
            for h in halves:
                term = lax.dot_general(
                    dv[h, plane],
                    slab[t * 256:(t + 1) * 256, h * HALF:(h + 1) * HALF],
                    (((1,), (1,)), ((), ())),
                    preferred_element_type=F32,
                )
                total = term if total is None else total + term
            if first:
                iacc[:, at] = total
            else:
                iacc[:, at] += total

    teach1.own()
    tasks = [functools.partial(student, n) for n in range(16)]
    tasks.append(functools.partial(teacher, 0, 0, 0))

    def run(count):
        for _ in range(count):
            if tasks:
                tasks.pop(0)()

    for n, f in enumerate(teach0.events()):
        f()
        tasks += [functools.partial(teacher, 0, *c) for c in DONE_AFTER.get(n, ())]
        run(1)
    for d in (1, 3, 2):
        tasks.append(functools.partial(f_arrived, d))
    tasks.append(functools.partial(finish_half, 0))
    tasks.append(functools.partial(teacher, 1, 0, 0))
    tail = []
    for n, f in enumerate(teach1.events()):
        f()
        tasks += [functools.partial(teacher, 1, *c) for c in DONE_AFTER.get(n, ())]
        run(2)
        if n == 15:
            d_forward(0)
    run(len(tasks))
    finish_half(1)

    row = jnp.sum(jnp.transpose(wcol[...]), axis=0, keepdims=True)
    sqv[0] = jnp.broadcast_to(row, (8, TOK))

    def q_copy(d):
        return remote(sqv.at[0], sqv.at[d], q_send.at[d - 1], q_recv.at[d - 1], zpeer(d))

    for d in (1, 2, 3):
        go(q_copy(d))
    d_last(0)
    for r in range(3):
        f_sib(r, 1 - core).wait_recv()
    for d in (1, 2, 3):
        q_copy(d).wait_recv()
    squares = sqv[0] + sqv[1] + sqv[2] + sqv[3]
    weight = 1.0 / (squares / QW + 1e-05)
    scale = 1.0 / math.sqrt(TOKENS)
    wcol[...] = jnp.transpose(jnp.broadcast_to(weight[0:1], (128, TOK)))
    for h in (0, 1):
        for t in range(4):
            g = wcol[...] * acc_s[h, :, t * 128:(t + 1) * 128] * scale
            gt[h * HALF + t * 128:h * HALF + (t + 1) * 128, :] = jnp.transpose(g).astype(BF16)

    def s_copy(dx, dy):
        at = rel(dx, dy)
        return remote(ss.at[at], sr.at[at], g_send.at[at], g_recv.at[at], env.sibling)

    def grads(dx, dy):
        chip = env.chip(dx, dy)
        cx, cy = mod4(x, dx), mod4(y, dy)
        for cc in (0, 1):
            full = jnp.dot(
                gt[...],
                xv[:, pl.ds(pl.multiple_of(chip * 512 + cc * 256, 256), 256)],
                preferred_element_type=F32,
            ).astype(BF16)
            for q in range(16):
                dense[cc, q] = full[q % 8 * BLK:(q % 8 + 1) * BLK, q // 8 * BLK:(q // 8 + 1) * BLK]
        for out, cc in ((ss, 1 - core), (pv, core)):
            for s in range(CAP):
                out[rel(dx, dy), s * BLK:(s + 1) * BLK, :] = dense[cc, idxs[cc, cy, cx, z, 0, s]]
        go(s_copy(dx, dy))

    def merge(dx, dy):
        s_copy(dx, dy).wait_recv()
        at = rel(dx, dy)
        pv[at] = (pv[at].astype(F32) + sr[at].astype(F32)).astype(BF16)

    def lane_off(lane, du, dv_):
        return (du, dv_) if lane == 0 else (dv_, du)

    def rows_of(lane, q0, nq):
        return pl.ds((lane * 2 + q0) * 192, nq * 192)

    def hop(lane, axis, sign):
        return env.peer(*lane_off(lane, sign, 0)) if axis == 0 else env.peer(*lane_off(lane, 0, sign))

    def v1_copy(lane, k, side):
        at = rel(*lane_off(lane, U_OF_K[k], 2))
        n = lane * 16 + k * 4 + side
        return remote(
            pv.at[at, rows_of(lane, side, 1), :], rv1.at[lane, k, side], r_send.at[n], r_recv.at[n],
            hop(lane, 1, 1 - 2 * side),
        )

    def v2_copy(lane, k, side):
        at = rel(*lane_off(lane, U_OF_K[k], 1 - 2 * side))
        n = lane * 16 + k * 4 + 2 + side
        return remote(
            pv.at[at, rows_of(lane, 0, 2), :], rv2.at[lane, k, side], r_send.at[n], r_recv.at[n],
            hop(lane, 1, 1 - 2 * side),
        )

    def u1_copy(lane, side):
        at = rel(*lane_off(lane, 2, 0))
        n = 32 + lane * 4 + side
        return remote(
            pv.at[at, rows_of(lane, side, 1), :], ru1.at[lane, side], r_send.at[n], r_recv.at[n],
            hop(lane, 0, 1 - 2 * side),
        )

    def u2_copy(lane, side):
        at = rel(*lane_off(lane, 1 - 2 * side, 0))
        n = 32 + lane * 4 + 2 + side
        return remote(
            pv.at[at, rows_of(lane, 0, 2), :], ru2.at[lane, side], r_send.at[n], r_recv.at[n],
            hop(lane, 0, 1 - 2 * side),
        )

    def add(at, lane, q0, nq, got):
        rows = rows_of(lane, q0, nq)
        pv[at, rows, :] = (pv[at, rows, :].astype(F32) + got.astype(F32)).astype(BF16)

    def rv_first(lane, k):
        for side in (0, 1):
            go(v1_copy(lane, k, side))

    def rv_second(lane, k):
        for side in (0, 1):
            v1_copy(lane, k, side).wait_recv()
            add(rel(*lane_off(lane, U_OF_K[k], 1 - 2 * side)), lane, side, 1, rv1[lane, k, side])
            go(v2_copy(lane, k, side))

    def rv_third(lane, k):
        for side in (0, 1):
            v2_copy(lane, k, side).wait_recv()
        at = rel(*lane_off(lane, U_OF_K[k], 0))
        add(at, lane, 0, 2, rv2[lane, k, 0].astype(F32) + rv2[lane, k, 1].astype(F32))

    def ru_first(lane):
        for side in (0, 1):
            go(u1_copy(lane, side))

    def ru_second(lane):
        for side in (0, 1):
            u1_copy(lane, side).wait_recv()
            add(rel(*lane_off(lane, 1 - 2 * side, 0)), lane, side, 1, ru1[lane, side])
            go(u2_copy(lane, side))

    def ru_third(lane):
        for side in (0, 1):
            u2_copy(lane, side).wait_recv()
        total = pv[0, rows_of(lane, 0, 2), :].astype(F32) + ru2[lane, 0].astype(F32) + ru2[lane, 1].astype(F32)
        for s in range(3):
            gout[lane * 3 + s, 0] = jnp.transpose(total[s * BLK:(s + 1) * BLK])

    lanes = lambda f, *a: [functools.partial(f, 0, *a), functools.partial(f, 1, *a)]
    after = {
        0: lanes(rv_first, 3),
        4: lanes(rv_first, 2) + lanes(rv_first, 1),
        6: lanes(rv_second, 3) + lanes(rv_first, 0),
        8: [],
        10: lanes(rv_second, 2) + lanes(rv_second, 1) + lanes(rv_third, 3) + lanes(ru_first),
        12: [],
        14: lanes(rv_second, 0) + lanes(rv_third, 2) + lanes(rv_third, 1) + lanes(ru_second),
    }
    for n, c in enumerate(GRAD_ORDER):
        grads(*c)
        if n > 0:
            merge(*GRAD_ORDER[n - 1])
            for f in after.get(n - 1, ()):
                f()
        if n == 6:
            d_forward(1)
    merge(*GRAD_ORDER[15])

    for n in range(4):
        input_grad(n, 0, (0, 1), True)
    for f in lanes(rv_third, 0):
        f()
    for n in range(4):
        input_grad(n, 1, (0, 1), False)
        input_grad(n, 3, (0, 1), False)
    d_last(1)
    for n in range(4):
        input_grad(n, 2, (0, 1), False)
    for n in range(16):
        at = slice(n * 128, (n + 1) * 128)
        iout[:, at] = (iacc[:, at] * (wcol[...] * scale)).astype(BF16)
    for f in lanes(ru_third):
        f()
    for c in env.started:
        c.wait_send()


def body(hidden_states, teacher_weight, student_blocks, block_index):
    listed = block_index[:, 0]
    slot = jnp.arange(16, dtype=jnp.int32)
    hit = listed[:, None] == slot[None, :]
    order = jnp.arange(CAP, dtype=jnp.int32)
    pick = jnp.min(jnp.where(hit, order[:, None], CAP), axis=0).astype(jnp.int32)
    places = jnp.concatenate(
        [jnp.where(listed < 0, 16, listed), jnp.zeros((2,), jnp.int32), pick, jnp.zeros((104,), jnp.int32)]
    ).reshape(1, 128)
    any_spec = pl.BlockSpec(memory_space=pl.ANY)
    vmem_spec = pl.BlockSpec(memory_space=pltpu.VMEM)
    dma = pltpu.SemaphoreType.DMA
    block_grads, input_grad = pl.pallas_call(
        kernel,
        out_shape=(
            jax.ShapeDtypeStruct((CAP, 1, BLK, BLK), F32),
            jax.ShapeDtypeStruct((TOK, OWN_COLS), BF16),
        ),
        in_specs=[any_spec] * 4,
        out_specs=(vmem_spec, vmem_spec),
        scratch_shapes=[
            pltpu.VMEM((TOK, D), BF16),
            pltpu.VMEM((2, 16, 2, 256, HALF), BF16),
            pltpu.VMEM((16, 2, BROWS, BLK), BF16),
            pltpu.VMEM((3, 4, 2, BROWS, BLK), BF16),
            pltpu.VMEM((2, 4, 4, 4, 1, 128), jnp.int32),
            pltpu.SMEM((2, 4, 4, 4, 1, 128), jnp.int32),
            pltpu.VMEM((2, TOK, HALF), F32),
            pltpu.VMEM((2, TOK, HALF), F32),
            pltpu.VMEM((2, CAP + 1, BLK, BLK), BF16),
            pltpu.VMEM((512, COLS), BF16),
            pltpu.VMEM((2, 4, TOK, HALF), BF16),
            pltpu.VMEM((COLS, TOK), BF16),
            pltpu.VMEM((2, 17, BLK, BLK), BF16),
            pltpu.VMEM((16, BROWS, BLK), BF16),
            pltpu.VMEM((16, BROWS, BLK), BF16),
            pltpu.VMEM((16, BROWS, BLK), BF16),
            pltpu.VMEM((2, 4, 2, 192, BLK), BF16),
            pltpu.VMEM((2, 4, 2, 384, BLK), BF16),
            pltpu.VMEM((2, 2, 192, BLK), BF16),
            pltpu.VMEM((2, 2, 384, BLK), BF16),
            pltpu.VMEM((4, 8, TOK), F32),
            pltpu.VMEM((TOK, 128), F32),
            pltpu.VMEM((TOK, OWN_COLS), F32),
            dma((6,)),
            dma((3, 2, 20)),
            dma((3, 2, 20)),
            dma((3, 32)),
            dma((3, 32)),
            dma((10,)),
            dma((10,)),
            dma((9,)),
            dma((9,)),
            dma((2, 4)),
            dma((2, 4)),
            dma((3,)),
            dma((3,)),
            dma((16,)),
            dma((16,)),
            dma((40,)),
            dma((40,)),
        ],
        compiler_params=pltpu.CompilerParams(
            collective_id=0, has_side_effects=True, vmem_limit_bytes=63 * 1024 * 1024
        ),
        cost_estimate=pl.CostEstimate(flops=26 * 10**9, bytes_accessed=10 * 10**6, transcendentals=0),
    )(hidden_states, teacher_weight, student_blocks.reshape(BROWS, BLK), places)
    return block_grads, input_grad


def solution(mesh):
    in_specs = (P("dp", None), P("dp", "tensor"), P("dp", "tensor", None, None), P("dp", "tensor"))
    out_specs = (P("dp", "tensor", None, None), P("dp", "tensor"))
    return jax.shard_map(body, mesh=mesh, in_specs=in_specs, out_specs=out_specs, check_vma=False)
```

time: 358 us -> 139 us (0.39)
  waiting for transfers between devices: 145 us -> 0 us
  Pallas kernels: 0 us -> 132 us
  local copies, waits for them, and re-layouts: 68.3 us -> 4.5 us
  matrix products: 55.3 us -> 0 us
  other arithmetic: 49.7 us -> 1.99 us
  blocking collectives: 23.7 us -> 0 us
  between operations: 14.5 us -> 0.64 us
    reduce_scatter x2 -> x0, waiting for transfers between devices: 137 us -> none  [the longest x1 70.8 us: body(): lax.psum_scatter(term[:, None].astype(jnp.bfloat16), 'dp', scatter_dimens...]
    pallas_call x0 -> x1, Pallas kernels: none -> 132 us  [body(): pl.pallas_call(kernel, out_shape=(jax.ShapeDtypeStruct((CAP, 1, BLK, BLK)...]
    dot_general x4 -> x0, matrix products: 55.3 us -> none  [the longest x1 18.1 us: body(): jnp.einsum('tkd,tke->kde', left, right, preferred_element_type=jnp.float32)]
    scatter-add x1 -> x0, other arithmetic: 40.1 us -> none  [scatter_blocks(): grid = grid.at[rows, :, cols, :].add(masked)]
    gather x2 -> x0, local copies, waits for them, and re-layouts: 24.2 us -> none  [the longest x1 13.9 us: body(): left = jnp.take(inputs3, rows, axis=1)]
    scatter-add x1 -> x0, local copies, waits for them, and re-layouts: 19.7 us -> none  [scatter_blocks(): grid = grid.at[rows, :, cols, :].add(masked)]
    unnamed x1 -> x0, blocking collectives: 14.9 us -> none
    psum x1 -> x0, blocking collectives: 8.8 us -> none  [body(): squares = lax.psum(squares, 'tensor')]
  transfers between devices with their start and end apart: 4 -> 0, of which waited for: 3 -> 0; matrix products, arithmetic and copies ran while one was open for 36% -> 0% of each run, Pallas kernels for 0% -> 0%
where the time goes in v1:
time: 139 us
  Pallas kernels  132 us (95%)
  local copies, waits for them, and re-layouts  4.5 us (3%)
  other arithmetic  1.99 us (1%)
    pallas_call x1, Pallas kernels, body(): pl.pallas_call(kernel, out_shape=(jax.ShapeDtypeStruct((CAP, 1, BLK, BLK)...  132 us
    unnamed x2, local copies, waits for them, and re-layouts  4.49 us

profile of v1, /device:TPU:1, one launch (start us, length us, event | category | flops | bytes accessed | tf_op | source)
XLA Modules:
  0.0 138.7 jit_solution(7617111121867563150)
XLA Ops:
  0.6 0.7 select_reduce_fusion
  1.4 0.7 compare_select_fusion
  2.0 0.6 add_bitcast_fusion.i_hbm
  2.6 131.6 %shard_map.59 = (f32[6,1,128,128]{3,2,1,0:T(8,128)}, bf16[384,2048]{1,0:T(8,128)(2,1)}) custom-call(bf16[384,8192]{1,0:T(8,128)(2,1)} %x_hbm.1, bf16[256,1024]{1,0:T(8,128)(2,1)} %w_hbm.1, bf16[768,128]{1,0:T(8,128)(2,1)} %bitcast.5, s32[1,128]{1,0:T(1,128)} %add_bitcast_fusion.i_hbm), custom_call_target="tpu_custom_call" | custom-call | flops 25999998976 | bytes 10000000 | tf_op jit(solution)/shard_map/pallas_call | solution.py:588
  134.2 1.8 %copy.8 = f32[6,1,128,128]{3,2,1,0:T(8,128)} copy(f32[6,1,128,128]{3,2,1,0:T(8,128)} %get-tuple-element.4) | data formatting | bytes 786432
  136.0 2.7 %copy.9 = bf16[384,2048]{1,0:T(8,128)(2,1)} copy(bf16[384,2048]{1,0:T(8,128)(2,1)} %get-tuple-element.5) | data formatting | bytes 3145728
  (2 shorter events, 0.0 us)
